TPU v7x, 512 devices: a whole 4x4x16 slice. The times are simulated.
512 devices in a mesh: dp: 4 (over y), tenant: 8 (over x, core), mp: 16 (over z).
Axes of the slice: x: 4, y: 4, z: 16, core: 2. Of those that a mesh axis runs over, the one named last changes fastest.
Arguments:
- cross_in: bfloat16 [32768, 3456], P(('dp', 'tenant'), 'mp'), may hold values from -6 to 6
- rank_act: bfloat16 [32768, 512], P(('dp', 'tenant')), may hold values from -6 to 6
- tower_cot: bfloat16 [32768, 1024], P(('dp', 'tenant')), may hold values from -6 to 6
- tenant_ids: int32 [32768, 1], P(('dp', 'tenant')), may hold values from 0 to 31; in each aligned block of 1024 rows (0 to 1023, 1024 to 2047, ...) at most 40 rows name the same one
- sparse_ids: int32 [32768, 26], P(('dp', 'tenant')), may hold values from 0 to 1023
- table_slot: int32 [26], replicated, may hold values from 0 to 31, as said below
- cross_u: bfloat16 [3456, 512], P('mp'), may hold values from -0.25 to 0.25
- cross_v: bfloat16 [3456, 512], P('mp'), may hold values from -0.109375 to 0.109375
- cross_bias: float32 [3456], P('mp'), may hold values from -1 to 1
- tower_w: bfloat16 [32, 3456, 1024], P(('dp', 'tenant'), 'mp'), may hold values from -0.1875 to 0.1875
Outputs:
- tower_wgrad: bfloat16 [32, 3456, 1024], P(('dp', 'tenant'), 'mp')
- cross_ugrad: float32 [3456, 512], P('mp')
- cross_vgrad: float32 [3456, 512], P('mp')
- cross_bgrad: float32 [3456], P('mp')
- table_grad: bfloat16 [32, 32, 1024, 128], P(('dp', 'tenant'), 'mp')
Inputs may be any that keep to these rules, and one draw needn't show every extreme that they name: `tenant_ids`: in each aligned block of 1024 rows (one sample group) no tenant is named more than 40 times, a bound that some block reaches. `table_slot`: distinct slots for distinct tables.
All inputs are finite; a program needn't handle non-finite values.
Results may differ from a plain program's by a relative error of at most 0.007.
Values may be sent and summed in bfloat16 or wider, within the bound.
A program may use at most 64 MiB of HBM per device.

v0:
```python
import math

import jax
import jax.numpy as jnp
from jax import lax
from jax.sharding import PartitionSpec as P

EMB = 128
VOCAB = 1024


def on_device(
    cross_in,
    rank_act,
    tower_cot,
    tenant_ids,
    sparse_ids,
    table_slot,
    cross_u,
    cross_v,
    cross_bias,
    tower_w,
):
    groups = lax.axis_size(("dp", "tenant"))
    model_size = lax.axis_size("mp")
    model_index = lax.axis_index("mp")
    samples_here = cross_in.shape[0]
    width_here = cross_in.shape[1]
    table_count = table_slot.shape[0]
    slot_count = (table_count + model_size - 1) // model_size
    capacity = (5 * samples_here + 4 * groups - 1) // (4 * groups)
    total_slots = groups * capacity
    grad_scale = 1.0 / math.sqrt(samples_here * groups)
    tenant = tenant_ids[:, 0]
    member = (tenant[:, None] == jnp.arange(groups, dtype=jnp.int32)[None, :]).astype(jnp.int32)
    before = jnp.cumsum(member, axis=0) - member
    position = jnp.sum(before * member, axis=1)
    target = tenant * capacity + position
    source_row = (
        jnp.zeros((total_slots,), jnp.int32)
        .at[target]
        .set(jnp.arange(samples_here, dtype=jnp.int32))
    )
    filled = jnp.zeros((total_slots,), jnp.bfloat16).at[target].set(1.0)

    def bucket(row_data):
        picked = jnp.take(row_data, source_row, axis=0) * filled[:, None]
        return picked.reshape(groups, capacity, row_data.shape[1])

    got_slices, got_rank, got_cot = (
        lax.all_to_all(bucket(cross_in), ("dp", "tenant"), split_axis=0, concat_axis=0, tiled=True),
        lax.all_to_all(bucket(rank_act), ("dp", "tenant"), split_axis=0, concat_axis=0, tiled=True),
        lax.all_to_all(
            bucket(tower_cot), ("dp", "tenant"), split_axis=0, concat_axis=0, tiled=True
        ),
    )
    got_slices = got_slices.reshape(total_slots, width_here)
    got_rank = got_rank.reshape(total_slots, -1)
    got_cot = got_cot.reshape(total_slots, -1)
    rank_up = jnp.einsum("rk,fk->rf", got_rank, cross_u, preferred_element_type=jnp.float32)
    shifted = rank_up + cross_bias[None, :]
    slices_wide = got_slices.astype(jnp.float32)
    crossed = (slices_wide * shifted + slices_wide).astype(jnp.bfloat16)
    tower_grad = jnp.einsum("rf,rh->fh", crossed, got_cot, preferred_element_type=jnp.float32)
    tower_wgrad = (tower_grad * grad_scale).astype(jnp.bfloat16)[None]
    back_grad = jnp.einsum("rh,fh->rf", got_cot, tower_w[0], preferred_element_type=jnp.float32)
    gate_grad = (back_grad * slices_wide).astype(jnp.bfloat16)
    rank_terms = jnp.einsum("rf,fk->rk", gate_grad, cross_u, preferred_element_type=jnp.float32)
    rank_grad = lax.psum(rank_terms, "mp")
    rank_round = rank_grad.astype(jnp.bfloat16)
    input_grad = (
        back_grad * (shifted + 1.0)
        + jnp.einsum("rk,fk->rf", rank_round, cross_v, preferred_element_type=jnp.float32)
    ).astype(jnp.bfloat16)
    u_terms = jnp.einsum("rf,rk->fk", gate_grad, got_rank, preferred_element_type=jnp.float32)
    v_terms = jnp.einsum("rf,rk->fk", got_slices, rank_round, preferred_element_type=jnp.float32)
    bias_terms = jnp.sum(gate_grad.astype(jnp.float32), axis=0)
    u_total, v_total, bias_total = lax.psum((u_terms, v_terms, bias_terms), ("dp", "tenant"))
    returned = lax.all_to_all(
        lax.all_to_all(
            input_grad.reshape(groups, capacity, width_here),
            ("dp", "tenant"),
            split_axis=0,
            concat_axis=0,
            tiled=True,
        ),
        "mp",
        split_axis=0,
        concat_axis=2,
        tiled=True,
    )
    owner_part = returned.shape[0]
    blocks = returned.reshape(owner_part, capacity, table_count + 1, EMB)[:, :, 1:, :]
    placing = (
        table_slot[:, None] == jnp.arange(model_size * slot_count, dtype=jnp.int32)[None, :]
    ).astype(jnp.bfloat16)
    slotted = jnp.einsum(
        "abte,ts->abse", blocks, placing, preferred_element_type=jnp.float32
    ).astype(jnp.bfloat16)
    landed = lax.all_to_all(slotted, "mp", split_axis=2, concat_axis=0, tiled=True)
    pooled = landed.reshape(total_slots, slot_count, EMB)
    row_ids = jnp.take(sparse_ids, source_row, axis=0)
    own_slots = model_index * slot_count + jnp.arange(slot_count, dtype=jnp.int32)
    choose = (table_slot[:, None] == own_slots[None, :]).astype(jnp.int32)
    slot_ids = jnp.dot(row_ids, choose)
    onehot = (slot_ids[:, :, None] == jnp.arange(VOCAB, dtype=jnp.int32)[None, None, :]).astype(
        jnp.bfloat16
    )
    table_sum = jnp.einsum("rkv,rke->kve", onehot, pooled, preferred_element_type=jnp.float32)
    table_grad = (table_sum * grad_scale).astype(jnp.bfloat16)[None]
    return (
        tower_wgrad,
        u_total * grad_scale,
        v_total * grad_scale,
        bias_total * grad_scale,
        table_grad,
    )


def solution(mesh):
    return jax.shard_map(
        on_device,
        mesh=mesh,
        in_specs=(
            P(("dp", "tenant"), "mp"),
            P(("dp", "tenant"), None),
            P(("dp", "tenant"), None),
            P(("dp", "tenant"), None),
            P(("dp", "tenant"), None),
            P(),
            P("mp", None),
            P("mp", None),
            P("mp"),
            P(("dp", "tenant"), "mp", None),
        ),
        out_specs=(
            P(("dp", "tenant"), "mp", None),
            P("mp", None),
            P("mp", None),
            P("mp"),
            P(("dp", "tenant"), "mp", None, None),
        ),
        check_vma=False,
    )
```

profile of v0, /device:TPU:1, one launch (start us, length us, event | category | flops | bytes accessed | tf_op | source)
XLA Modules:
  0.0 448.0 jit_solution(420144670306226406)
XLA Ops:
  7.2 0.9 fusion.25
  8.1 9.0 %reduce-window.6 = s32[32,8,128]{2,1,0:T(8,128)S(1)} reduce-window(s32[32,8,128]{2,1,0:T(8,128)S(1)} %fusion.25, s32[]{:T(128)} %constant.35.clone.1), window={size=1x1x128 pad=0_0x0_0x127_0}, to_apply=%region_0.0 | reduce-window | flops 4161536 | bytes 262148 | tf_op jit(solution)/shard_map/reduce-window
  17.2 0.1 copy.28
  17.4 0.1 broadcast_add_fusion
  17.5 0.7 fusion.24
  18.3 0.7 compare_select_fusion
  19.0 4.3 scatter_custom_fusion
  23.4 7.6 %scatter_custom_fusion.1 = bf16[1280]{0:T(1024)(128)(2,1)S(1)} fusion(s32[1024]{0:T(1024)S(1)} %bitcast.85, bf16[1024]{0:T(1024)(128)(2,1)S(1)} %broadcast.55, bf16[]{:T(256)} %constant.47.clone.1), kind=kCustom, calls=%fused_computation.61 | custom fusion | bytes 2562 | tf_op jit(solution)/shard_map/scatter | solution.py:44
  31.1 0.2 copy.30
  31.3 4.7 %gather_fusion = bf16[1280,216]{1,0:T(8,128)(2,1)} fusion(bf16[1024,216]{1,0:T(8,128)(2,1)S(1)} %copy.30, s32[2048]{0:T(1024)S(1)} %pad_clamp_fusion), kind=kCustom, calls=%fused_computation | custom fusion | bytes 1111040 | tf_op jit(solution)/shard_map/jit(_take)/gather | solution.py:47
  36.0 2.4 select_multiply_fusion.2
  38.4 11.1 %all-to-all-start = ((bf16[32,40,216]{2,1,0:T(8,128)(2,1)}), bf16[32,40,216]{2,1,0:T(8,128)(2,1)}, u32[]{:S(2)}, u32[]{:S(2)}) async-start(bf16[32,40,216]{2,1,0:T(8,128)(2,1)} %select_multiply_fusion.2), calls=%async_computation | async-start | bytes 1310720 | tf_op jit(solution)/shard_map/all_to_all | solution.py:51
  49.5 4.7 %gather_fusion.1 = bf16[1280,512]{1,0:T(8,128)(2,1)} fusion(bf16[1024,512]{1,0:T(8,128)(2,1)S(1)} %copy-done.1, s32[2048]{0:T(1024)S(1)} %pad_clamp_fusion), kind=kCustom, calls=%fused_computation.1 | custom fusion | bytes 2626560 | tf_op jit(solution)/shard_map/jit(_take)/gather | solution.py:47
  54.2 2.4 select_multiply_fusion.1
  56.7 5.9 %all-to-all-done = bf16[32,40,216]{2,1,0:T(8,128)(2,1)} async-done(((bf16[32,40,216]{2,1,0:T(8,128)(2,1)}), bf16[32,40,216]{2,1,0:T(8,128)(2,1)}, u32[]{:S(2)}, u32[]{:S(2)}) %all-to-all-start) | async-done | bytes 552992 | tf_op jit(solution)/shard_map/all_to_all | solution.py:51
  62.6 4.1 all-to-all-start.1
  66.8 5.1 %gather_fusion.2 = bf16[1280,1024]{1,0:T(8,128)(2,1)} fusion(bf16[1024,1024]{1,0:T(8,128)(2,1)S(1)} %copy-done, s32[2048]{0:T(1024)S(1)} %pad_clamp_fusion), kind=kCustom, calls=%fused_computation.2 | custom fusion | bytes 5248000 | tf_op jit(solution)/shard_map/jit(_take)/gather | solution.py:47
  71.8 3.1 select_multiply_fusion
  74.9 11.0 %all-to-all-done.1 = bf16[32,40,512]{2,1,0:T(8,128)(2,1)S(1)} async-done(((bf16[32,40,512]{2,1,0:T(8,128)(2,1)}), bf16[32,40,512]{2,1,0:T(8,128)(2,1)S(1)}, u32[]{:S(2)}, u32[]{:S(2)}) %all-to-all-start.1) | async-done | bytes 1310752 | tf_op jit(solution)/shard_map/all_to_all | solution.py:52
  85.9 6.4 %all-to-all-start.2 = ((bf16[32,40,1024]{2,1,0:T(8,128)(2,1)}), bf16[32,40,1024]{2,1,0:T(8,128)(2,1)}, u32[]{:S(2)}, u32[]{:S(2)}) async-start(bf16[32,40,1024]{2,1,0:T(8,128)(2,1)} %select_multiply_fusion), calls=%async_computation.2 | async-start | bytes 5242880 | tf_op jit(solution)/shard_map/all_to_all | solution.py:53
  92.3 2.1 copy.31
  94.4 2.5 convolution_add_fusion.1
  96.9 29.0 %all-to-all-done.2 = bf16[32,40,1024]{2,1,0:T(8,128)(2,1)} async-done(((bf16[32,40,1024]{2,1,0:T(8,128)(2,1)}), bf16[32,40,1024]{2,1,0:T(8,128)(2,1)}, u32[]{:S(2)}, u32[]{:S(2)}) %all-to-all-start.2) | async-done | bytes 2621472 | tf_op jit(solution)/shard_map/all_to_all | solution.py:53
  126.0 4.1 convert_reduce_fusion
  130.1 0.8 copy-done.5
  130.9 2.1 fusion.39
  132.9 70.9 %all-reduce.5 = bf16[1280,512]{1,0:T(8,128)(2,1)S(1)} all-reduce(f32[1280,512]{1,0:T(8,128)} %fusion.39), channel_id=1, replica_groups=mesh['dp'=4,'tenant'=8,'mp'=16] {'mp'}, use_global_device_ids=true, to_apply=%region_6.7 | all-reduce | flops 655360 | bytes 3932160 | tf_op jit(solution)/shard_map/psum | solution.py:69
  203.8 3.5 fusion.2
  207.3 2.1 copy.33
  209.5 29.4 %all_to_all.50 = bf16[32,40,216]{2,1,0:T(8,128)(2,1)S(1)} all-to-all(bf16[32,40,216]{2,1,0:T(8,128)(2,1)} %bitcast.74), channel_id=1, replica_groups=mesh['dp'=4,'tenant'=8,'mp'=16] {'dp','tenant'}, dimensions={0} | all-to-all | bytes 1105920 | tf_op jit(solution)/shard_map/all_to_all | solution.py:80
  238.9 41.5 %all_to_all.51 = bf16[32,40,216]{2,1,0:T(8,128)(2,1)S(1)} all-to-all(bf16[32,40,216]{2,1,0:T(8,128)(2,1)S(1)} %all_to_all.50), channel_id=1, replica_groups=mesh['dp'=4,'tenant'=8,'mp'=16] {'mp'}, dimensions={0} | all-to-all | bytes 1105920 | tf_op jit(solution)/shard_map/all_to_all | solution.py:79
  280.4 0.2 copy.41
  280.6 2.7 reshape.97
  283.3 0.3 fusion.6
  283.7 1.1 copy.35
  284.7 7.1 %all-to-all-start.5 = ((bf16[2,40,32,128]{3,1,0,2:T(8,128)(2,1)}), bf16[2,40,32,128]{3,1,0,2:T(8,128)(2,1)}, u32[]{:S(2)}, u32[]{:S(2)}) async-start(bf16[2,40,32,128]{3,1,0,2:T(8,128)(2,1)} %copy.35), calls=%async_computation.5 | async-start | bytes 1310720 | tf_op jit(solution)/shard_map/all_to_all | solution.py:100
  291.9 0.2 copy.32
  292.1 3.2 gather_fusion.3
  295.3 1.7 fusion.12
  297.0 2.6 fusion.38
  299.7 2.4 fusion.40
  302.1 63.9 %psum.31 = f32[216]{0:T(256)S(1)} all-reduce(f32[216]{0:T(256)S(1)} %get-tuple-element.7), channel_id=1, replica_groups=mesh['dp'=4,'tenant'=8,'mp'=16] {'dp','tenant'}, use_global_device_ids=true, to_apply=%region_9.10 | all-reduce | flops 216 | bytes 1728 | tf_op jit(solution)/shard_map/psum | solution.py:78
  366.0 0.6 broadcast_multiply_fusion.2
  366.6 3.4 fusion.8
  370.0 65.2 %all-reduce.4.cloned.1.call-done = (f32[216,512]{1,0:T(8,128)}, f32[216,512]{1,0:T(8,128)}) async-done(((f32[216,512]{1,0:T(8,128)}, f32[216,512]{1,0:T(8,128)}), (f32[216,512]{1,0:T(8,128)}, f32[216,512]{1,0:T(8,128)})) %all-reduce.4.cloned.1.call-update) | async-done | bytes 884752 | tf_op jit(solution)/shard_map/psum | solution.py:78
  435.3 2.1 broadcast_multiply_fusion
  437.4 1.1 copy.36
  438.6 2.6 fusion.7
  (40 shorter events, 0.5 us)
Async XLA Ops:
  7.2 59.6 %copy-start = (bf16[1024,1024]{1,0:T(8,128)(2,1)S(1)}, bf16[1024,1024]{1,0:T(8,128)(2,1)}, u32[]{:S(2)}) copy-start(bf16[1024,1024]{1,0:T(8,128)(2,1)} %param.12) | copy-start | bytes 6291460
  7.2 23.9 %copy-start.9 = (bf16[1024,216]{0,1:T(8,128)(2,1)S(1)}, bf16[1024,216]{0,1:T(8,128)(2,1)}, u32[]{:S(2)}) copy-start(bf16[1024,216]{0,1:T(8,128)(2,1)} %param.10) | copy-start | bytes 1327108
  36.0 13.5 %copy-start.1 = (bf16[1024,512]{1,0:T(8,128)(2,1)S(1)}, bf16[1024,512]{1,0:T(8,128)(2,1)}, u32[]{:S(2)}) copy-start(bf16[1024,512]{1,0:T(8,128)(2,1)} %param.11) | copy-start | bytes 3145732
  38.4 24.2 %all-to-all-start = ((bf16[32,40,216]{2,1,0:T(8,128)(2,1)}), bf16[32,40,216]{2,1,0:T(8,128)(2,1)}, u32[]{:S(2)}, u32[]{:S(2)}) async-start(bf16[32,40,216]{2,1,0:T(8,128)(2,1)} %select_multiply_fusion.2), calls=%async_computation | async-start | bytes 1310720 | tf_op jit(solution)/shard_map/all_to_all | solution.py:51
  62.6 23.3 %all-to-all-start.1 = ((bf16[32,40,512]{2,1,0:T(8,128)(2,1)}), bf16[32,40,512]{2,1,0:T(8,128)(2,1)S(1)}, u32[]{:S(2)}, u32[]{:S(2)}) async-start(bf16[32,40,512]{2,1,0:T(8,128)(2,1)} %select_multiply_fusion.1), calls=%async_computation.1 | async-start | bytes 2621440 | tf_op jit(solution)/shard_map/all_to_all | solution.py:52
  74.9 19.5 %copy-start.12 = (f32[216]{0:T(256)S(1)}, f32[216]{0:T(256)}, u32[]{:S(2)}) copy-start(f32[216]{0:T(256)} %param.18) | copy-start | bytes 2596
  85.9 8.5 %copy-start.2 = (bf16[32,40,512]{2,1,0:T(8,128)(2,1)}, bf16[32,40,512]{2,1,0:T(8,128)(2,1)S(1)}, u32[]{:S(2)}) copy-start(bf16[32,40,512]{2,1,0:T(8,128)(2,1)S(1)} %all-to-all-done.1) | copy-start | bytes 3932164
  85.9 40.1 %all-to-all-start.2 = ((bf16[32,40,1024]{2,1,0:T(8,128)(2,1)}), bf16[32,40,1024]{2,1,0:T(8,128)(2,1)}, u32[]{:S(2)}, u32[]{:S(2)}) async-start(bf16[32,40,1024]{2,1,0:T(8,128)(2,1)} %select_multiply_fusion), calls=%async_computation.2 | async-start | bytes 5242880 | tf_op jit(solution)/shard_map/all_to_all | solution.py:53
  126.0 4.9 %copy-start.8 = (bf16[216,512]{1,0:T(8,128)(2,1)S(1)}, bf16[216,512]{1,0:T(8,128)(2,1)}, u32[]{:S(2)}) copy-start(bf16[216,512]{1,0:T(8,128)(2,1)} %param.16) | copy-start | bytes 663556
  130.1 0.8 copy-start.5
  203.8 3.5 copy-start.3
  280.4 2.9 copy-start.11
  283.6 8.2 %copy-start.10 = (s32[1024,26]{0,1:T(8,128)S(1)}, s32[1024,26]{0,1:T(8,128)}, u32[]{:S(2)}) copy-start(s32[1024,26]{0,1:T(8,128)} %param.14) | copy-start | bytes 319492
  284.7 152.7 %all-to-all-start.5 = ((bf16[2,40,32,128]{3,1,0,2:T(8,128)(2,1)}), bf16[2,40,32,128]{3,1,0,2:T(8,128)(2,1)}, u32[]{:S(2)}, u32[]{:S(2)}) async-start(bf16[2,40,32,128]{3,1,0,2:T(8,128)(2,1)} %copy.35), calls=%async_computation.5 | async-start | bytes 1310720 | tf_op jit(solution)/shard_map/all_to_all | solution.py:100
  291.8 143.5 %all-reduce.4.cloned.1.call-start = ((), (), s32[]{:S(2)}) async-start(), calls=%async_computation.6 | async-start | bytes 1769472 | tf_op jit(solution)/shard_map/psum | solution.py:78
  292.1 4.9 %copy-start.6 = (bf16[1280,216]{0,1:T(8,128)(2,1)S(1)}, bf16[1280,216]{0,1:T(8,128)(2,1)}, u32[]{:S(2)}) copy-start(bf16[1280,216]{0,1:T(8,128)(2,1)} %copy-done.5) | copy-start | bytes 1658884
  297.0 2.7 copy-start.4
  299.7 66.9 %copy-start.7 = (f32[1280,216]{0,1:T(8,128)S(1)}, f32[1280,216]{0,1:T(8,128)}, u32[]{:S(2)}) copy-start(f32[1280,216]{0,1:T(8,128)} %convolution_add_fusion.1) | copy-start | bytes 3317764
Sparse Core Ops, SparseCore 0:
  302.2 133.0 all-reduce.3
where the time goes:
time: 449 us; the launch traced here: 448 us
  blocking collectives  206 us (46%)
  waiting for transfers between devices  111 us (25%)
  local copies, waits for them, and re-layouts  40.7 us (9%)
  starting transfers between devices  28.7 us (6%)
  matrix products  25.3 us (6%)
  other arithmetic  22.1 us (5%)
  between operations  14.3 us (3%)
    psum x1, blocking collectives, on_device(): rank_grad = lax.psum(rank_terms, 'mp')  70.9 us
    psum x1, waiting for transfers between devices, on_device(): lax.psum((u_terms, v_terms, bias_terms), ('dp', 'tenant'))  65.2 us
    psum x1, blocking collectives, on_device(): lax.psum((u_terms, v_terms, bias_terms), ('dp', 'tenant'))  63.9 us
    all_to_all x1, blocking collectives, on_device(): lax.all_to_all(lax.all_to_all(input_grad.reshape(groups, capacity, width_...  41.5 us
    all_to_all x1, blocking collectives, on_device(): lax.all_to_all(input_grad.reshape(groups, capacity, width_here), ('dp', '...  29.4 us
    all_to_all x1, waiting for transfers between devices, on_device(): lax.all_to_all(bucket(tower_cot), ('dp', 'tenant'), split_axis=0, concat_...  29 us
    gather x3, local copies, waits for them, and re-layouts, bucket(): picked = jnp.take(row_data, source_row, axis=0) * filled[:, None]  14.4 us
    all_to_all x1, starting transfers between devices, on_device(): lax.all_to_all(bucket(cross_in), ('dp', 'tenant'), split_axis=0, concat_a...  11.1 us
  transfers between devices with their start and end apart: 5, of which 4 were waited for; matrix products, arithmetic and copies ran while one was open for 8% of the time, Pallas kernels for 0%

commit v1 on v0

v1 whole, which is shorter than its diff:
```python
import functools
import math

import jax
import jax.numpy as jnp
from jax import lax
from jax.experimental import pallas as pl
from jax.experimental.pallas import tpu as pltpu
from jax.sharding import PartitionSpec as P

EMB = 128
VOCAB = 1024
WIDE = 256
MESH = pl.DeviceIdType.MESH
F32 = jnp.float32
BF16 = jnp.bfloat16


def mm(a, b):
    return jnp.dot(a, b, preferred_element_type=F32)


def mm_nt(a, b):
    return lax.dot_general(a, b, (((1,), (1,)), ((), ())), preferred_element_type=F32)


def mm_tn(a, b):
    return lax.dot_general(a, b, (((0,), (0,)), ((), ())), preferred_element_type=F32)


def fused(
    nd,
    nt,
    nz,
    cap,
    scale,
    inv_ref,
    ids_ref,
    xin_ref,
    rank_ref,
    cot_ref,
    u_ref,
    v_ref,
    bias_ref,
    w_ref,
    wg_out,
    u_out,
    v_out,
    b_out,
    tab_out,
    uv,
    xinp,
    crp,
    wp,
    tgt,
    perm_t,
    send,
    got,
    cotr,
    crr,
    rsend,
    rgot,
    backb,
    bh,
    gate_h,
    xgot,
    bgot,
    shift,
    rr_all,
    igp,
    igs,
    s5,
    tgot,
    hot,
    part,
    pgot,
    pred,
    pall,
    a_send,
    a_recv,
    r_send,
    r_recv,
    x_send,
    x_recv,
    b_send,
    b_recv,
    uv_send,
    uv_recv,
    sib_send,
    sib_recv,
    rr_send,
    rr_recv,
    t_send,
    t_recv,
    p_send,
    p_recv,
    q_send,
    q_recv,
):
    groups = nd * nt
    rows, width = xin_ref.shape
    rank = rank_ref.shape[1]
    half_rank = rank // 2
    hid = cot_ref.shape[1]
    half_hid = hid // 2
    chunk = rows // nz
    block = nt * cap
    uv_rows = (width + 3 + 15) // 16 * 16
    base = width // 16 * 16
    piece = WIDE // groups
    slots = tab_out.shape[0]

    dp = lax.axis_index("dp")
    tn = lax.axis_index("tenant")
    mp = lax.axis_index("mp")
    me = dp * nt + tn
    core = lax.rem(tn, 2)

    def plane(peer):
        return (peer // nt, lax.rem(peer, nt), mp)

    def column(z):
        return (dp, tn, z)

    def remote(src, dst, ssem, rsem, device):
        return pltpu.make_async_remote_copy(
            src_ref=src,
            dst_ref=dst,
            send_sem=ssem,
            recv_sem=rsem,
            device_id=device,
            device_id_type=MESH,
        )

    uv[:, :, 0, base:, :] = jnp.zeros((nz, 2, WIDE - base, half_rank), BF16)

    barrier = pltpu.get_barrier_semaphore()

    def greet_plane(o, carry):
        pl.semaphore_signal(barrier, inc=1, device_id=plane(lax.rem(me + o, groups)), device_id_type=MESH)
        return carry

    def greet_column(o, carry):
        pl.semaphore_signal(barrier, inc=1, device_id=column(lax.rem(mp + o, nz)), device_id_type=MESH)
        return carry

    lax.fori_loop(1, groups, greet_plane, 0)
    lax.fori_loop(1, nz, greet_column, 0)

    bias = jnp.concatenate([bias_ref[...], jnp.zeros((1, WIDE - width), F32)], axis=1)
    hi = bias.astype(BF16).astype(F32)
    mid = (bias - hi).astype(BF16).astype(F32)
    low = bias - hi - mid
    bias_rows = [hi, mid, low, jnp.zeros((uv_rows - width - 3, WIDE), F32)]
    for h in range(2):
        cols = slice(h * half_rank, (h + 1) * half_rank)
        uv[mp, h, 0, 0:base] = u_ref[0:base, cols]
        tail = bias_rows
        if base < width:
            tail = [u_ref[base:width, cols].astype(F32)] + bias_rows
        uv[mp, h, 0, base:uv_rows] = jnp.concatenate(tail, axis=0).astype(BF16)
        uv[mp, h, 1, 0:width] = v_ref[:, cols]
    xinp[:, 0:128] = xin_ref[:, 0:128]
    xinp[:, 128:WIDE] = jnp.concatenate(
        [xin_ref[:, 128:width].astype(F32), jnp.zeros((rows, WIDE - width), F32)], axis=1
    ).astype(BF16)
    whole = (width - 1) // 16 * 16
    wp[0:whole] = w_ref[0:whole]
    wp[whole:WIDE] = jnp.concatenate(
        [w_ref[whole:width].astype(F32), jnp.zeros((WIDE - width, hid), F32)], axis=0
    ).astype(BF16)

    tenant = ids_ref[0:1, :]
    member = lax.broadcasted_iota(jnp.int32, (groups, rows), 0) == tenant
    earlier = lax.broadcasted_iota(jnp.int32, (rows, rows), 0) < lax.broadcasted_iota(
        jnp.int32, (rows, rows), 1
    )
    before = mm(member.astype(F32).astype(BF16), earlier.astype(F32).astype(BF16))
    position = jnp.sum(jnp.where(member, before, 0.0), axis=0, keepdims=True)
    target = tenant * cap + position.astype(jnp.int32)
    tgt[...] = jnp.broadcast_to(target, tgt.shape)

    pl.semaphore_wait(barrier, groups - 1 + nz - 1)

    right, left = lax.rem(mp + 1, nz), lax.rem(mp + nz - 1, nz)
    sibling = (dp, tn + 1 - 2 * core, mp)
    half_ring = nz // 2

    def uv_copy(c, way, step):
        spot = uv.at[c, core, :, 0:uv_rows]
        return remote(spot, spot, uv_send.at[way, step], uv_recv.at[c], column(right if way == 0 else left))

    def sib_copy(c):
        spot = uv.at[c, core, :, 0:uv_rows]
        return remote(spot, spot, sib_send.at[c], sib_recv.at[c], sibling)

    def uv_ring(step):
        came = lax.rem(mp + nz - step, nz)
        uv_copy(came, 0, step - 1).wait_recv()

        @pl.when(step < half_ring)
        def _():
            uv_copy(came, 0, step).start()

        sib_copy(came).start()

        @pl.when(step < half_ring)
        def _():
            other = lax.rem(mp + step, nz)
            uv_copy(other, 1, step - 1).wait_recv()

            @pl.when(step < half_ring - 1)
            def _():
                uv_copy(other, 1, step).start()

            sib_copy(other).start()

    uv_copy(mp, 0, 0).start()
    uv_copy(mp, 1, 0).start()

    rank_up = mm_nt(rank_ref[:, 0:half_rank], uv[mp, 0, 0]) + mm_nt(
        rank_ref[:, half_rank:rank], uv[mp, 1, 0]
    )
    wide = xinp[...].astype(F32)
    crp[...] = (wide * (rank_up + bias) + wide).astype(BF16)

    def a_copy(peer, source):
        return remote(send.at[peer], got.at[source], a_send.at[peer], a_recv.at[source], plane(peer))

    def bucket(k, carry):
        to = lax.rem(dp + k, nd)
        chosen = lax.broadcasted_iota(jnp.int32, (block, rows), 0) + to * block == tgt[0:1, :]
        chosen = chosen.astype(F32).astype(BF16)
        cots = mm(chosen, cot_ref[...])
        crossed = mm(chosen, crp[...])
        for j in range(nt):
            s = slice(j * cap, (j + 1) * cap)
            send[to * nt + j] = jnp.concatenate(
                [
                    jnp.concatenate([cots[s, 0:half_hid], crossed[s, 0:128]], axis=1),
                    jnp.concatenate([cots[s, half_hid:hid], crossed[s, 128:WIDE]], axis=1),
                ],
                axis=0,
            ).astype(BF16)

        def start(o, inner):
            peer = to * nt + lax.rem(tn + o, nt)

            @pl.when(peer != me)
            def _():
                a_copy(peer, me).start()

            return inner

        lax.fori_loop(0, nt, start, 0)
        return carry

    lax.fori_loop(0, nd, bucket, 0)
    got[me] = send[me]

    target_col = jnp.transpose(tgt[...].astype(F32))[:, 0:1].astype(jnp.int32)
    perm_t[...] = (
        (lax.broadcasted_iota(jnp.int32, perm_t.shape, 1) == target_col).astype(F32).astype(BF16)
    )

    uv_ring(1)

    def x_copy(z, source):
        return remote(
            xinp.at[pl.ds(pl.multiple_of(z * chunk, chunk), chunk)],
            xgot.at[source],
            x_send.at[z],
            x_recv.at[source],
            column(z),
        )

    def each_z(body):
        def run(o, carry):
            body(lax.rem(mp + o, nz))
            return carry

        lax.fori_loop(1, nz, run, 0)

    def each_peer(body):
        def run(o, carry):
            body(lax.rem(me + o, groups))
            return carry

        lax.fori_loop(1, groups, run, 0)

    each_z(lambda z: x_copy(z, mp).start())
    xgot[mp] = xinp[pl.ds(pl.multiple_of(mp * chunk, chunk), chunk)]

    def r_copy(peer, source):
        return remote(rsend.at[peer], rgot.at[source], r_send.at[peer], r_recv.at[source], plane(peer))

    def owner(k, carry):
        frm = lax.rem(dp + nd - k, nd)

        @pl.when(k + 2 <= half_ring)
        def _():
            uv_ring(k + 2)

        def arrive(o, inner):
            peer = frm * nt + o

            @pl.when(peer != me)
            def _():
                a_copy(me, peer).wait_recv()

            return inner

        lax.fori_loop(0, nt, arrive, 0)
        cots, crossed = [], []
        for j in range(nt):
            blk = got[frm * nt + j].astype(F32)
            cots.append(jnp.concatenate([blk[0:cap, 0:half_hid], blk[cap:, 0:half_hid]], axis=1))
            crossed.append(jnp.concatenate([blk[0:cap, half_hid:], blk[cap:, half_hid:]], axis=1))
        cots = jnp.concatenate(cots, axis=0).astype(BF16)
        at = pl.ds(pl.multiple_of(frm * block, block), block)
        cotr[at] = cots
        crr[at] = jnp.concatenate(crossed, axis=0).astype(BF16)
        back = mm_nt(cots, wp[...])
        for j in range(nt):
            s = slice(j * cap, (j + 1) * cap)
            rsend[frm * nt + j] = jnp.concatenate(
                [back[s, 0:128], back[s, 128:WIDE]], axis=0
            ).astype(BF16)

        def start(o, inner):
            peer = frm * nt + lax.rem(tn + o, nt)

            @pl.when(peer != me)
            def _():
                r_copy(peer, me).start()

            return inner

        lax.fori_loop(0, nt, start, 0)
        return carry

    lax.fori_loop(0, nd, owner, 0)
    rgot[me] = rsend[me]

    wgrad = mm_tn(crr[...], cotr[...])
    wg_out[...] = (wgrad[0:width] * scale).astype(BF16)

    each_peer(lambda p: r_copy(me, p).wait_recv())

    def unpack(t, carry):
        pair = []
        for j in range(2):
            blk = rgot[2 * t + j].astype(F32)
            pair.append(jnp.concatenate([blk[0:cap], blk[cap:]], axis=1))
        backb[pl.ds(pl.multiple_of(t * 2 * cap, 2 * cap), 2 * cap)] = jnp.concatenate(
            pair, axis=0
        ).astype(BF16)
        return carry

    lax.fori_loop(0, groups // 2, unpack, 0)
    bh[...] = mm(perm_t[...], backb[...]).astype(BF16)

    def b_copy(z, source):
        return remote(
            bh.at[pl.ds(pl.multiple_of(z * chunk, chunk), chunk)],
            bgot.at[source],
            b_send.at[z],
            b_recv.at[source],
            column(z),
        )

    each_z(lambda z: b_copy(z, mp).start())
    bgot[mp] = bh[pl.ds(pl.multiple_of(mp * chunk, chunk), chunk)]

    def p_copy(i, peer, source):
        return remote(
            part.at[i, pl.ds(pl.multiple_of(peer * piece, piece), piece)],
            pgot.at[i, source],
            p_send.at[i, peer],
            p_recv.at[i, source],
            plane(peer),
        )

    def q_copy(i, peer, source):
        return remote(
            pred.at[i],
            pall.at[i, pl.ds(pl.multiple_of(source * piece, piece), piece)],
            q_send.at[i, peer],
            q_recv.at[i, source],
            plane(peer),
        )

    def scatter(i):
        each_peer(lambda p: p_copy(i, p, me).start())
        pgot[i, me] = part[i, pl.ds(pl.multiple_of(me * piece, piece), piece)]

    def gather(i):
        each_peer(lambda p: p_copy(i, me, p).wait_recv())
        total = jnp.sum(pgot[i], axis=0) * scale
        pred[i] = total
        pall[i, pl.ds(pl.multiple_of(me * piece, piece), piece)] = total
        each_peer(lambda p: q_copy(i, p, me).start())

    gate_h[...] = (bh[...].astype(F32) * xinp[...].astype(F32)).astype(BF16)
    part[0] = mm_tn(gate_h[...], rank_ref[...])
    part[0, width : width + 8, 0:WIDE] = mm(jnp.ones((8, rows), BF16), gate_h[...])
    scatter(0)

    for step in range(nd + 2, half_ring + 1):
        uv_ring(step)
    each_z(lambda z: sib_copy(z).wait_recv())

    rank_here = rank_ref[pl.ds(pl.multiple_of(mp * chunk, chunk), chunk), :]

    def shift_of(z, carry):
        ends = uv[z, 0, 0, base:uv_rows].astype(F32)
        first = width - base
        bias_z = ends[first : first + 1] + ends[first + 1 : first + 2] + ends[first + 2 : first + 3]
        up = mm_nt(rank_here[:, 0:half_rank], uv[z, 0, 0]) + mm_nt(
            rank_here[:, half_rank:rank], uv[z, 1, 0]
        )
        shift[z] = up + bias_z + 1.0
        return carry

    lax.fori_loop(0, nz, shift_of, 0)

    for k in range(slots):
        table = inv_ref[mp * slots + k]
        ids = jnp.sum(
            jnp.where(lax.broadcasted_iota(jnp.int32, ids_ref.shape, 0) == table, ids_ref[...], 0),
            axis=0,
            keepdims=True,
        )
        hot[k] = (lax.broadcasted_iota(jnp.int32, (VOCAB, rows), 0) == ids).astype(F32).astype(BF16)

    gather(0)

    each_z(lambda z: x_copy(mp, z).wait_recv())
    each_z(lambda z: b_copy(mp, z).wait_recv())

    def rank_of(z, total):
        gate = (bgot[z].astype(F32) * xgot[z].astype(F32)).astype(BF16)
        return total[0] + mm(gate, uv[z, 0, 0]), total[1] + mm(gate, uv[z, 1, 0])

    zero = jnp.zeros((chunk, half_rank), F32)
    lo, up = lax.fori_loop(0, nz, rank_of, (zero, zero))
    rr = jnp.concatenate([lo, up], axis=1).astype(BF16)
    rr_all[mp] = rr

    def rr_copy(c, way, step):
        return remote(
            rr_all.at[c],
            rr_all.at[c],
            rr_send.at[way, step],
            rr_recv.at[c],
            column(right if way == 0 else left),
        )

    rr_copy(mp, 0, 0).start()
    rr_copy(mp, 1, 0).start()

    def input_of(z, carry):
        igp[z] = bgot[z].astype(F32) * shift[z] + (
            mm_nt(rr[:, 0:half_rank], uv[z, 0, 1]) + mm_nt(rr[:, half_rank:rank], uv[z, 1, 1])
        )
        return carry

    lax.fori_loop(0, nz, input_of, 0)
    igs[0] = jnp.zeros((chunk, EMB), BF16)
    for t in range(1, igs.shape[0]):
        pieces, at = [], t * EMB
        while at < (t + 1) * EMB:
            z, first = at // width, at % width
            stop = min(width, first + (t + 1) * EMB - at)
            pieces.append(igp[z][:, first:stop])
            at += stop - first
        igs[t] = jnp.concatenate(pieces, axis=1).astype(BF16)

    def t_copy(z, source):
        return remote(s5.at[z], tgot.at[source], t_send.at[z], t_recv.at[source], column(z))

    def fill(z, carry):
        for k in range(slots):
            s5[z, k] = igs[inv_ref[z * slots + k]]
        return carry

    lax.fori_loop(0, nz, fill, 0)
    each_z(lambda z: t_copy(z, mp).start())
    tgot[mp] = s5[mp]

    def rr_ring(step, carry):
        came = lax.rem(mp + nz - step, nz)
        rr_copy(came, 0, step - 1).wait_recv()

        @pl.when(step < half_ring)
        def _():
            rr_copy(came, 0, step).start()
            other = lax.rem(mp + step, nz)
            rr_copy(other, 1, step - 1).wait_recv()

            @pl.when(step < half_ring - 1)
            def _():
                rr_copy(other, 1, step).start()

        return carry

    lax.fori_loop(1, half_ring + 1, rr_ring, 0)

    part[1] = mm_tn(xinp[...], rr_all[...].reshape(rows, rank))
    scatter(1)

    each_z(lambda z: t_copy(mp, z).wait_recv())
    for k in range(slots):
        values = tgot[:, k].reshape(rows, EMB)
        tab_out[k] = (mm(hot[k], values) * scale).astype(BF16)

    gather(1)
    for i, out in ((0, u_out), (1, v_out)):
        each_peer(lambda p: q_copy(i, me, p).wait_recv())
        out[...] = pall[i, 0:width]
    b_out[...] = pall[0, width : width + 1, 0:width]

    def left_plane(p):
        a_copy(p, me).wait_send()
        r_copy(p, me).wait_send()
        for i in range(2):
            p_copy(i, p, me).wait_send()
            q_copy(i, p, me).wait_send()

    def left_column(z):
        x_copy(z, mp).wait_send()
        b_copy(z, mp).wait_send()
        t_copy(z, mp).wait_send()
        sib_copy(z).wait_send()

    each_peer(left_plane)
    each_z(left_column)
    for step in range(half_ring):
        uv_copy(mp, 0, step).wait_send()
        rr_copy(mp, 0, step).wait_send()
        if step < half_ring - 1:
            uv_copy(mp, 1, step).wait_send()
            rr_copy(mp, 1, step).wait_send()


def on_device(
    cross_in,
    rank_act,
    tower_cot,
    tenant_ids,
    sparse_ids,
    table_slot,
    cross_u,
    cross_v,
    cross_bias,
    tower_w,
):
    nd, nt, nz = lax.axis_size("dp"), lax.axis_size("tenant"), lax.axis_size("mp")
    groups = nd * nt
    rows, width = cross_in.shape
    rank, hid = rank_act.shape[1], tower_cot.shape[1]
    tables = table_slot.shape[0]
    slots = (tables + nz - 1) // nz
    cap = (5 * rows + 4 * groups - 1) // (4 * groups)
    chunk = rows // nz
    half_ring = nz // 2
    scale = 1.0 / math.sqrt(rows * groups)

    taken = table_slot[:, None] == jnp.arange(nz * slots, dtype=jnp.int32)[None, :]
    numbers = jnp.arange(1, tables + 1, dtype=jnp.int32)[:, None]
    inverse = jnp.sum(jnp.where(taken, numbers, 0), axis=0)
    ids = jnp.concatenate([tenant_ids, sparse_ids], axis=1).T

    vmem = pl.BlockSpec(memory_space=pltpu.VMEM)
    smem = pl.BlockSpec(memory_space=pltpu.SMEM)
    sem = pltpu.SemaphoreType.DMA

    def bf(*shape):
        return pltpu.VMEM(shape, BF16)

    def ff(*shape):
        return pltpu.VMEM(shape, F32)

    out = pl.pallas_call(
        functools.partial(fused, nd, nt, nz, cap, scale),
        out_shape=(
            jax.ShapeDtypeStruct((width, hid), BF16),
            jax.ShapeDtypeStruct((width, rank), F32),
            jax.ShapeDtypeStruct((width, rank), F32),
            jax.ShapeDtypeStruct((1, width), F32),
            jax.ShapeDtypeStruct((slots, VOCAB, EMB), BF16),
        ),
        in_specs=[smem] + [vmem] * 8,
        out_specs=(vmem,) * 5,
        scratch_shapes=[
            bf(nz, 2, 2, WIDE, rank // 2),
            bf(rows, WIDE),
            bf(rows, WIDE),
            bf(WIDE, hid),
            pltpu.VMEM((8, rows), jnp.int32),
            bf(rows, groups * cap),
            bf(groups, 2 * cap, hid // 2 + 128),
            bf(groups, 2 * cap, hid // 2 + 128),
            bf(groups * cap, hid),
            bf(groups * cap, WIDE),
            bf(groups, 2 * cap, 128),
            bf(groups, 2 * cap, 128),
            bf(groups * cap, WIDE),
            bf(rows, WIDE),
            bf(rows, WIDE),
            bf(nz, chunk, WIDE),
            bf(nz, chunk, WIDE),
            ff(nz, chunk, WIDE),
            bf(nz, chunk, rank),
            ff(nz, chunk, WIDE),
            bf(tables + 1, chunk, EMB),
            bf(nz, slots, chunk, EMB),
            bf(nz, slots, chunk, EMB),
            bf(slots, VOCAB, rows),
            ff(2, WIDE, rank),
            ff(2, groups, WIDE // groups, rank),
            ff(2, WIDE // groups, rank),
            ff(2, WIDE, rank),
            sem((groups,)),
            sem((groups,)),
            sem((groups,)),
            sem((groups,)),
            sem((nz,)),
            sem((nz,)),
            sem((nz,)),
            sem((nz,)),
            sem((2, half_ring)),
            sem((nz,)),
            sem((nz,)),
            sem((nz,)),
            sem((2, half_ring)),
            sem((nz,)),
            sem((nz,)),
            sem((nz,)),
            sem((2, groups)),
            sem((2, groups)),
            sem((2, groups)),
            sem((2, groups)),
        ],
        compiler_params=pltpu.CompilerParams(
            collective_id=0, has_side_effects=True, vmem_limit_bytes=60 * 2**20
        ),
    )(
        inverse,
        ids,
        cross_in,
        rank_act,
        tower_cot,
        cross_u,
        cross_v,
        cross_bias[None, :],
        tower_w[0],
    )
    wgrad, u_total, v_total, b_total, table = out
    return wgrad[None], u_total, v_total, b_total[0], table[None]


def solution(mesh):
    return jax.shard_map(
        on_device,
        mesh=mesh,
        in_specs=(
            P(("dp", "tenant"), "mp"),
            P(("dp", "tenant"), None),
            P(("dp", "tenant"), None),
            P(("dp", "tenant"), None),
            P(("dp", "tenant"), None),
            P(),
            P("mp", None),
            P("mp", None),
            P("mp"),
            P(("dp", "tenant"), "mp", None),
        ),
        out_specs=(
            P(("dp", "tenant"), "mp", None),
            P("mp", None),
            P("mp", None),
            P("mp"),
            P(("dp", "tenant"), "mp", None, None),
        ),
        check_vma=False,
    )
```

time: 449 us -> 214 us (0.48)
  blocking collectives: 206 us -> 0 us
  Pallas kernels: 0 us -> 201 us
  waiting for transfers between devices: 111 us -> 0 us
  local copies, waits for them, and re-layouts: 40.7 us -> 8.84 us
  starting transfers between devices: 28.7 us -> 0 us
  matrix products: 25.3 us -> 0 us
  other arithmetic: 22.1 us -> 2.84 us
  between operations: 14.3 us -> 0.67 us
    pallas_call x0 -> x1, Pallas kernels: none -> 201 us  [on_device(): pl.pallas_call(functools.partial(fused, nd, nt, nz, cap, scale), out_shap...]
    psum x2 -> x0, blocking collectives: 135 us -> none  [the longest x1 70.9 us: on_device(): rank_grad = lax.psum(rank_terms, 'mp')]
    all_to_all x2 -> x0, blocking collectives: 70.9 us -> none  [the longest x1 41.5 us: on_device(): lax.all_to_all(lax.all_to_all(input_grad.reshape(groups, capacity, width_...]
    psum x1 -> x0, waiting for transfers between devices: 65.2 us -> none  [on_device(): lax.psum((u_terms, v_terms, bias_terms), ('dp', 'tenant'))]
    all_to_all x4 -> x0, waiting for transfers between devices: 46 us -> none  [the longest x1 29 us: on_device(): lax.all_to_all(bucket(tower_cot), ('dp', 'tenant'), split_axis=0, concat_...]
    all_to_all x4 -> x0, starting transfers between devices: 28.7 us -> none  [the longest x1 11.1 us: on_device(): lax.all_to_all(bucket(cross_in), ('dp', 'tenant'), split_axis=0, concat_a...]
    dot_general x10 -> x0, matrix products: 25.3 us -> none  [the longest x1 4.1 us: on_device(): jnp.einsum('rh,fh->rf', got_cot, tower_w[0], preferred_element_type=jnp.f...]
    gather x4 -> x0, local copies, waits for them, and re-layouts: 17.6 us -> none  [the longest x3 14.4 us: bucket(): picked = jnp.take(row_data, source_row, axis=0) * filled[:, None]]
  transfers between devices with their start and end apart: 5 -> 0, of which waited for: 4 -> 0; matrix products, arithmetic and copies ran while one was open for 8% -> 0% of each run, Pallas kernels for 0% -> 0%
where the time goes in v1:
time: 214 us
  Pallas kernels  201 us (94%)
  local copies, waits for them, and re-layouts  8.84 us (4%)
  other arithmetic  2.84 us (1%)
    pallas_call x1, Pallas kernels, on_device(): pl.pallas_call(functools.partial(fused, nd, nt, nz, cap, scale), out_shap...  201 us
    unnamed x10, local copies, waits for them, and re-layouts  8.84 us

profile of v1, /device:TPU:1, one launch (start us, length us, event | category | flops | bytes accessed | tf_op | source)
XLA Modules:
  0.0 213.7 jit_solution(6368318296021632756)
XLA Ops:
  0.6 1.3 select_reduce_fusion.inv_ref
  1.9 1.6 add_bitcast_fusion.ids_ref
  3.5 2.0 copy.16.xin_ref
  5.5 201.3 %shard_map.137 = (bf16[216,1024]{1,0:T(8,128)(2,1)}, f32[216,512]{1,0:T(8,128)}, f32[216,512]{1,0:T(8,128)}, f32[1,216]{1,0:T(1,128)}, bf16[2,1024,128]{2,1,0:T(8,128)(2,1)}) custom-call(s32[32]{0:T(128)} %select_reduce_fusion.inv_ref, s32[27,1024]{1,0:T(8,128)} %add_bitcast_fusion.ids_ref, bf16[1024,216]{1,0:T(8,128)(2,1)} %copy.16.xin_ref, ...), custom_call_target="tpu_custom_call" | custom-call | tf_op jit(solution)/shard_map/pallas_call | solution.py:584
  206.8 0.0 copy-start.1
  206.8 0.0 copy-start
  206.9 1.9 copy.22
  208.7 1.8 copy.23
  210.5 1.8 copy.24
  212.3 0.0 copy-done.1
  212.3 0.6 copy.25
  212.9 0.0 copy-done
  212.9 0.8 copy.26
  (1 shorter events, 0.0 us)
Async XLA Ops:
  206.8 5.5 %copy-start.1 = (f32[1,216]{1,0:T(1,128)S(1)}, f32[1,216]{1,0:T(1,128)}, u32[]{:S(2)}) copy-start(f32[1,216]{1,0:T(1,128)} %get-tuple-element.13) | copy-start | bytes 2596
  206.8 6.0 %copy-start = (bf16[2,1024,128]{2,1,0:T(8,128)(2,1)S(1)}, bf16[2,1024,128]{2,1,0:T(8,128)(2,1)}, u32[]{:S(2)}) copy-start(bf16[2,1024,128]{2,1,0:T(8,128)(2,1)} %get-tuple-element.14) | copy-start | bytes 1572868

commit v2 on v1

v2 whole, which is shorter than its diff:
```python
import functools
import math

import jax
import jax.numpy as jnp
from jax import lax
from jax.experimental import pallas as pl
from jax.experimental.pallas import tpu as pltpu
from jax.sharding import PartitionSpec as P

EMB = 128
VOCAB = 1024
T_SENT = (2, 4, 6, 8, 12)
WIDE = 256
MESH = pl.DeviceIdType.MESH
F32 = jnp.float32
BF16 = jnp.bfloat16


def mm(a, b):
    return jnp.dot(a, b, preferred_element_type=F32)


def mm_nt(a, b):
    return lax.dot_general(a, b, (((1,), (1,)), ((), ())), preferred_element_type=F32)


def mm_tn(a, b):
    return lax.dot_general(a, b, (((0,), (0,)), ((), ())), preferred_element_type=F32)


def fused(
    nd,
    nt,
    nz,
    cap,
    scale,
    slot_ref,
    tenant_hbm,
    xin_hbm,
    u_hbm,
    rank_hbm,
    bias_hbm,
    cot_hbm,
    v_hbm,
    w_hbm,
    ids_hbm,
    wg_hbm,
    u_out_hbm,
    v_out_hbm,
    b_out_hbm,
    tab_hbm,
    tenant_ref,
    xin_ref,
    u_ref,
    rank_ref,
    bias_ref,
    cot_ref,
    v_ref,
    w_ref,
    ids_ref,
    wg_out,
    tab_out,
    inv_ref,
    in_sem,
    out_sem,
    uo,
    bo,
    uv,
    up,
    vp,
    xin_t,
    xinp,
    crp,
    wp,
    tgt,
    perm_t,
    send,
    got,
    cotr,
    crr,
    rsend,
    rgot,
    backb,
    bh,
    gate_h,
    xgot,
    bgot,
    shift,
    rr_all,
    igp,
    igs,
    s5,
    tgot,
    hot,
    part,
    pgot,
    pred,
    pall,
    tally,
    a_send,
    a_recv,
    r_sem,
    x_sem,
    b_sem,
    uv_send,
    uv_recv,
    sib_send,
    sib_recv,
    swap_send,
    swap_recv,
    late_send,
    late_recv,
    rr_send,
    rr_recv,
    t_sem,
    p_sem,
    q_sem,
):
    groups = nd * nt
    width, rows = xin_ref.shape
    rank = rank_ref.shape[1]
    half_rank = rank // 2
    hid = cot_ref.shape[1]
    half_hid = hid // 2
    chunk = rows // nz
    block = nt * cap
    uv_rows = (width + 3 + 15) // 16 * 16
    base = width // 16 * 16
    piece = 2 * WIDE // groups
    per_half = groups // 2
    slots = tab_out.shape[0]

    dp = lax.axis_index("dp")
    tn = lax.axis_index("tenant")
    mp = lax.axis_index("mp")
    me = dp * nt + tn
    core = lax.rem(tn, 2)
    across = tn // 2
    nx = nt // 2

    def partner(o):
        k, a, c = o // (2 * nd), lax.rem(nd - lax.rem(o // 2, nd), nd), lax.rem(o, 2)
        there = lax.rem(across + a + k, nx)
        return lax.rem(dp + a, nd) * nt + 2 * there + lax.rem(core + c, 2)

    def plane(peer):
        return (peer // nt, lax.rem(peer, nt), mp)

    def column(z):
        return (dp, tn, z)

    def remote(src, dst, ssem, rsem, device):
        return pltpu.make_async_remote_copy(
            src_ref=src,
            dst_ref=dst,
            send_sem=ssem,
            recv_sem=rsem,
            device_id=device,
            device_id_type=MESH,
        )

    pairs = [
        (tenant_hbm, tenant_ref),
        (xin_hbm, xin_ref),
        (u_hbm, u_ref),
        (rank_hbm, rank_ref),
        (bias_hbm, bias_ref),
        (cot_hbm, cot_ref),
        (v_hbm, v_ref),
        (w_hbm, w_ref),
        (ids_hbm, ids_ref),
    ]
    loads = [pltpu.make_async_copy(a, b, in_sem.at[i]) for i, (a, b) in enumerate(pairs)]
    for load in loads:
        load.start()

    uv[:, :, 0, uv_rows:, :] = jnp.zeros((nz, 2, WIDE - uv_rows, half_rank), BF16)

    barrier = pltpu.get_barrier_semaphore()

    def greet_plane(o, carry):
        pl.semaphore_signal(barrier, inc=1, device_id=plane(lax.rem(me + o, groups)), device_id_type=MESH)
        return carry

    def greet_column(o, carry):
        pl.semaphore_signal(barrier, inc=1, device_id=column(lax.rem(mp + o, nz)), device_id_type=MESH)
        return carry

    lax.fori_loop(1, groups, greet_plane, 0)
    lax.fori_loop(1, nz, greet_column, 0)

    for load in loads[:5]:
        load.wait()

    bias = jnp.concatenate([bias_ref[...], jnp.zeros((1, WIDE - width), F32)], axis=1)
    hi = bias.astype(BF16).astype(F32)
    mid = (bias - hi).astype(BF16).astype(F32)
    low = bias - hi - mid
    bias_rows = [hi, mid, low, jnp.zeros((WIDE - width - 3, WIDE), F32)]
    for h in range(2):
        cols = slice(h * half_rank, (h + 1) * half_rank)
        up[h, 0:base] = u_ref[0:base, cols]
        tail = bias_rows
        if base < width:
            tail = [u_ref[base:width, cols].astype(F32)] + bias_rows
        up[h, base:WIDE] = jnp.concatenate(tail, axis=0).astype(BF16)
    whole = (width - 1) // 16 * 16

    def padded(ref):
        ends = ref[whole:width].astype(F32)
        ends = jnp.concatenate([ends, jnp.zeros((WIDE - width, ref.shape[1]), F32)], axis=0)
        return ends.astype(BF16)

    xin_t[0:whole] = xin_ref[0:whole]
    xin_t[whole:WIDE] = padded(xin_ref)
    xinp[...] = jnp.transpose(xin_t[...])

    tenant = tenant_ref[...]
    member = lax.broadcasted_iota(jnp.int32, (groups, rows), 0) == tenant
    earlier = lax.broadcasted_iota(jnp.int32, (rows, rows), 0) < lax.broadcasted_iota(
        jnp.int32, (rows, rows), 1
    )
    before = mm(member.astype(F32).astype(BF16), earlier.astype(F32).astype(BF16))
    position = jnp.sum(jnp.where(member, before, 0.0), axis=0, keepdims=True)
    target = tenant * cap + position.astype(jnp.int32)
    tgt[...] = jnp.broadcast_to(target, tgt.shape)

    pl.semaphore_wait(barrier, groups - 1 + nz - 1)

    right, left = lax.rem(mp + 1, nz), lax.rem(mp + nz - 1, nz)
    sibling = (dp, tn + 1 - 2 * core, mp)
    beside = (dp, lax.rem(across + 1, 2) * 2 + across // 2 * 4 + core, mp)
    above = (dp // 2 * 2 + 1 - lax.rem(dp, 2), tn, mp)
    half_ring = nz // 2

    half_rows = uv_rows // 2
    even = lax.rem(across + dp, 2)
    mine = pl.ds(pl.multiple_of(even * half_rows, half_rows), half_rows)
    others = pl.ds(pl.multiple_of((1 - even) * half_rows, half_rows), half_rows)

    class Both:
        def __init__(self, copies):
            self.copies = copies

        def start(self):
            for copy in self.copies:
                copy.start()

        def wait_recv(self):
            for copy in self.copies:
                copy.wait_recv()

        def wait_send(self):
            for copy in self.copies:
                copy.wait_send()

    def parts(c):
        return uv.at[c, core, 0, 0:uv_rows], uv.at[c, core, 1, mine]

    def uv_copy(c, way, step):
        to = column(right if way == 0 else left)
        return Both(
            [remote(x, x, uv_send.at[i, way, step], uv_recv.at[i, c], to) for i, x in enumerate(parts(c))]
        )

    def sib_copy(c):
        return Both(
            [remote(x, x, sib_send.at[i, c], sib_recv.at[i, c], sibling) for i, x in enumerate(parts(c))]
        )

    def swap_copy(i):
        spot = uv.at[i * half_ring : (i + 1) * half_ring, core, 1, mine]
        return remote(spot, spot, swap_send.at[i], swap_recv.at[i], above if i else beside)

    def late_copy(i):
        spot = uv.at[i * half_ring : (i + 1) * half_ring, core, 1, others]
        return remote(spot, spot, late_send.at[i], late_recv.at[i], sibling)

    def uv_ring(step):
        came = lax.rem(mp + nz - step, nz)
        uv_copy(came, 0, step - 1).wait_recv()

        @pl.when(step < half_ring)
        def _():
            uv_copy(came, 0, step).start()

        sib_copy(came).start()

        @pl.when(step < half_ring)
        def _():
            other = lax.rem(mp + step, nz)
            uv_copy(other, 1, step - 1).wait_recv()

            @pl.when(step < half_ring - 1)
            def _():
                uv_copy(other, 1, step).start()

            sib_copy(other).start()

    loads[6].wait()
    for h in range(2):
        vp[h, 0:whole] = v_ref[0:whole, h * half_rank : (h + 1) * half_rank]
        vp[h, whole:WIDE] = padded(v_ref)[:, h * half_rank : (h + 1) * half_rank]
    uv[mp, core, 0, 0:uv_rows] = up[core, 0:uv_rows]
    uv[mp, core, 1, mine] = vp[core, mine]
    uv_copy(mp, 0, 0).start()
    uv_copy(mp, 1, 0).start()
    sib_copy(mp).start()

    rank_up = mm_nt(rank_ref[:, 0:half_rank], up[0]) + mm_nt(rank_ref[:, half_rank:rank], up[1])
    wide = xinp[...].astype(F32)
    crp[...] = (wide * (rank_up + bias) + wide).astype(BF16)

    loads[5].wait()

    def drain(ref, count, sem):
        spot = ref.at[pl.ds(0, count)]
        pltpu.make_async_copy(spot, spot, sem).wait()

    def a_copy(peer, k):
        return remote(send.at[peer], got.at[me], a_send.at[0], a_recv.at[k], plane(peer))

    def tenants_of(k, way):
        first = []
        for a in range(nd):
            up = lax.rem(dp + nd + way * a, nd)
            there = lax.rem(across + 2 * nx + way * lax.rem(a + k, nx), nx)
            first.append(up * nt + 2 * there)
        return first

    def bucket(k, carry):
        firsts = tenants_of(k, 1)
        spots = lax.broadcasted_iota(jnp.int32, (2 * cap, rows), 0)
        chosen = jnp.concatenate([spots + first * cap for first in firsts], axis=0) == tgt[0:1, :]
        chosen = chosen.astype(F32).astype(BF16)
        cots = mm(chosen, cot_ref[...])
        crossed = mm(chosen, crp[...])
        for j in range(2 * nd):
            s = slice(j * cap, (j + 1) * cap)
            send[firsts[j // 2] + j % 2] = jnp.concatenate(
                [
                    jnp.concatenate([cots[s, 0:half_hid], crossed[s, 0:128]], axis=1),
                    jnp.concatenate([cots[s, half_hid:hid], crossed[s, 128:WIDE]], axis=1),
                ],
                axis=0,
            ).astype(BF16)

        def start(o, inner):
            peer = partner(k * 2 * nd + o)

            @pl.when(peer != me)
            def _():
                a_copy(peer, k).start()

            return inner

        lax.fori_loop(0, 2 * nd, start, 0)
        return carry

    lax.fori_loop(0, nx, bucket, 0)
    got[me] = send[me]

    target_col = jnp.transpose(tgt[...].astype(F32))[:, 0:1].astype(jnp.int32)
    perm_t[...] = (
        (lax.broadcasted_iota(jnp.int32, perm_t.shape, 1) == target_col).astype(F32).astype(BF16)
    )

    uv_ring(1)
    loads[7].wait()
    wp[0:whole] = w_ref[0:whole]
    wp[whole:WIDE] = padded(w_ref)
    uv_ring(2)

    tables = slot_ref.shape[0]

    def invert(slot, carry):
        number = jnp.int32(0)
        for t in range(tables):
            number = jnp.where(slot_ref[t] == slot, t + 1, number)
        inv_ref[slot] = number
        return carry

    lax.fori_loop(0, nz * slots, invert, 0)
    loads[8].wait()
    for k in range(slots):
        table = inv_ref[mp * slots + k] - 1
        ids = jnp.sum(
            jnp.where(lax.broadcasted_iota(jnp.int32, ids_ref.shape, 0) == table, ids_ref[...], 0),
            axis=0,
            keepdims=True,
        )
        hot[k] = (lax.broadcasted_iota(jnp.int32, (VOCAB, rows), 0) == ids).astype(F32).astype(BF16)

    uv_ring(3)

    def x_copy(z):
        here = pl.ds(pl.multiple_of(z * chunk, chunk), chunk)
        return remote(xinp.at[here], xgot.at[mp], x_sem.at[0], x_sem.at[1], column(z))

    def each_z(body):
        def run(o, carry):
            step = (o + 1) // 2
            body(lax.rem(mp + jnp.where(lax.rem(o, 2) == 1, step, nz - step), nz))
            return carry

        lax.fori_loop(1, nz, run, 0)

    def each_peer(body):
        def run(o, carry):
            body(partner(o))
            return carry

        lax.fori_loop(1, groups, run, 0)

    xgot[mp] = xinp[pl.ds(pl.multiple_of(mp * chunk, chunk), chunk)]

    def r_copy(peer):
        return remote(rsend.at[peer], rgot.at[me], r_sem.at[0], r_sem.at[1], plane(peer))

    for step in range(4, half_ring + 1):
        uv_ring(step)
    for i in range(2):
        swap_copy(i).start()

    each_z(lambda z: x_copy(z).start())

    def owner(k, carry):
        firsts = tenants_of(k, -1)

        @pl.when(k == 0)
        def _():
            drain(got, 2 * nd - 1, a_recv.at[0])

        @pl.when(k > 0)
        def _():
            drain(got, 2 * nd, a_recv.at[k])

        cots, crossed = [], []
        for first in firsts:
            for j in range(2):
                blk = got[first + j].astype(F32)
                cots.append(jnp.concatenate([blk[0:cap, 0:half_hid], blk[cap:, 0:half_hid]], axis=1))
                crossed.append(jnp.concatenate([blk[0:cap, half_hid:], blk[cap:, half_hid:]], axis=1))
        cots = jnp.concatenate(cots, axis=0).astype(BF16)
        at = pl.ds(pl.multiple_of(k * 2 * nd * cap, 2 * nd * cap), 2 * nd * cap)
        cotr[at] = cots
        crr[at] = jnp.concatenate(crossed, axis=0).astype(BF16)
        back = mm_nt(cots, wp[...])
        for j in range(2 * nd):
            s = slice(j * cap, (j + 1) * cap)
            rsend[firsts[j // 2] + j % 2] = jnp.concatenate(
                [back[s, 0:128], back[s, 128:WIDE]], axis=0
            ).astype(BF16)
        for first in firsts:
            for j in range(2):

                @pl.when(first + j != me)
                def _():
                    r_copy(first + j).start()

        return carry

    lax.fori_loop(0, nx, owner, 0)
    rgot[me] = rsend[me]

    wgrad = mm_tn(crr[...], cotr[...])
    wg_out[...] = (wgrad[0:width] * scale).astype(BF16)
    stores = [
        pltpu.make_async_copy(wg_out, wg_hbm, out_sem.at[0]),
        pltpu.make_async_copy(uo.at[0], u_out_hbm, out_sem.at[1]),
        pltpu.make_async_copy(uo.at[1], v_out_hbm, out_sem.at[2]),
        pltpu.make_async_copy(bo, b_out_hbm, out_sem.at[3]),
        pltpu.make_async_copy(tab_out, tab_hbm, out_sem.at[4]),
    ]
    stores[0].start()

    drain(rgot, groups - 1, r_sem.at[1])

    def unpack(t, carry):
        pair = []
        for j in range(2):
            blk = rgot[2 * t + j].astype(F32)
            pair.append(jnp.concatenate([blk[0:cap], blk[cap:]], axis=1))
        backb[pl.ds(pl.multiple_of(t * 2 * cap, 2 * cap), 2 * cap)] = jnp.concatenate(
            pair, axis=0
        ).astype(BF16)
        return carry

    lax.fori_loop(0, groups // 2, unpack, 0)
    bh[...] = mm(perm_t[...], backb[...]).astype(BF16)

    def b_copy(z):
        here = pl.ds(pl.multiple_of(z * chunk, chunk), chunk)
        return remote(bh.at[here], bgot.at[mp], b_sem.at[0], b_sem.at[1], column(z))

    each_z(lambda z: b_copy(z).start())
    bgot[mp] = bh[pl.ds(pl.multiple_of(mp * chunk, chunk), chunk)]

    def piece_of(peer):
        return peer // per_half, pl.ds(pl.multiple_of(lax.rem(peer, per_half) * piece, piece), piece)

    def p_copy(i, peer):
        h, at = piece_of(peer)
        return remote(part.at[i, h, at], pgot.at[i, me], p_sem.at[i, 0], p_sem.at[i, 1], plane(peer))

    def q_copy(i, peer):
        h, at = piece_of(me)
        return remote(pred.at[i], pall.at[i, h, at], q_sem.at[i, 0], q_sem.at[i, 1], plane(peer))

    def scatter(i):
        each_peer(lambda p: p_copy(i, p).start())
        h, at = piece_of(me)
        pgot[i, me] = part[i, h, at]

    def gather(i):
        drain(pgot.at[i], groups - 1, p_sem.at[i, 1])
        pred[i] = (jnp.sum(pgot[i], axis=0) * scale).astype(BF16)
        each_peer(lambda p: q_copy(i, p).start())
        h, at = piece_of(me)
        pall[i, h, at] = pred[i]

    def gathered(i):
        drain(tally, (groups - 1) * piece, q_sem.at[i, 1])
        for h in range(2):
            uo[i, :, h * half_rank : (h + 1) * half_rank] = pall[i, h, 0:width].astype(F32)

    gate_h[...] = (bh[...].astype(F32) * xinp[...].astype(F32)).astype(BF16)
    u_part = mm_tn(gate_h[...], rank_ref[...])
    for h in range(2):
        part[0, h] = u_part[:, h * half_rank : (h + 1) * half_rank]
    part[0, 0, width : width + 8] = mm(jnp.ones((8, rows), BF16), gate_h[...])
    scatter(0)

    for z in range(nz):
        sib_copy(z).wait_recv()

    rank_here = rank_ref[pl.ds(pl.multiple_of(mp * chunk, chunk), chunk), :]

    def shift_of(z, carry):
        ends = uv[z, 0, 0, base:uv_rows].astype(F32)
        first = width - base
        bias_z = ends[first : first + 1] + ends[first + 1 : first + 2] + ends[first + 2 : first + 3]
        up = mm_nt(rank_here[:, 0:half_rank], uv[z, 0, 0]) + mm_nt(
            rank_here[:, half_rank:rank], uv[z, 1, 0]
        )
        shift[z] = up + bias_z + 1.0
        return carry

    lax.fori_loop(0, nz, shift_of, 0)
    for i in range(2):
        swap_copy(i).wait_recv()
        late_copy(i).start()
    gather(0)

    drain(xgot, nz - 1, x_sem.at[1])
    drain(bgot, nz - 1, b_sem.at[1])

    def rank_of(z, total):
        gate = (bgot[z].astype(F32) * xgot[z].astype(F32)).astype(BF16)
        return total[0] + mm(gate, uv[z, 0, 0]), total[1] + mm(gate, uv[z, 1, 0])

    zero = jnp.zeros((chunk, half_rank), F32)
    lo, up = lax.fori_loop(0, nz, rank_of, (zero, zero))
    rr = jnp.concatenate([lo, up], axis=1).astype(BF16)
    rr_all[mp] = rr

    def rr_copy(c, way, step):
        return remote(
            rr_all.at[c],
            rr_all.at[c],
            rr_send.at[way, step],
            rr_recv.at[c],
            column(right if way == 0 else left),
        )

    rr_copy(mp, 0, 0).start()
    rr_copy(mp, 1, 0).start()

    def rr_ring(step):
        came = lax.rem(mp + nz - step, nz)
        rr_copy(came, 0, step - 1).wait_recv()

        @pl.when(step < half_ring)
        def _():
            rr_copy(came, 0, step).start()
            other = lax.rem(mp + step, nz)
            rr_copy(other, 1, step - 1).wait_recv()

            @pl.when(step < half_ring - 1)
            def _():
                rr_copy(other, 1, step).start()

    def input_of(z, carry):
        igp[z] = bgot[z].astype(F32) * shift[z] + (
            mm_nt(rr[:, 0:half_rank], uv[z, 0, 1]) + mm_nt(rr[:, half_rank:rank], uv[z, 1, 1])
        )
        return carry

    for i in range(2):
        late_copy(i).wait_recv()
    lax.fori_loop(0, nz // 2, input_of, 0)
    rr_ring(1)
    lax.fori_loop(nz // 2, nz, input_of, 0)
    rr_ring(2)
    igs[0] = jnp.zeros((chunk, EMB), BF16)
    for t in range(1, igs.shape[0]):
        pieces, at = [], t * EMB
        while at < (t + 1) * EMB:
            z, first = at // width, at % width
            stop = min(width, first + (t + 1) * EMB - at)
            pieces.append(igp[z][:, first:stop])
            at += stop - first
        igs[t] = jnp.concatenate(pieces, axis=1).astype(BF16)

    def t_copy(z):
        return remote(s5.at[z], tgot.at[mp], t_sem.at[0], t_sem.at[1], column(z))

    def fill(z, carry):
        for k in range(slots):
            s5[z, k] = igs[inv_ref[z * slots + k]]
        return carry

    lax.fori_loop(0, nz, fill, 0)
    sent = 0
    for step in range(3, half_ring + 1):
        rr_ring(step)
        upto = nz - 1 if step == half_ring else min(nz - 1, T_SENT[step - 3])
        for o in range(sent + 1, upto + 1):
            t_copy(lax.rem(mp + ((o + 1) // 2 if o % 2 else nz - o // 2), nz)).start()
        sent = upto
    tgot[mp] = s5[mp]

    v_part = mm(xin_t[...], rr_all[...].reshape(rows, rank))
    for h in range(2):
        part[1, h] = v_part[:, h * half_rank : (h + 1) * half_rank]
    scatter(1)
    gathered(0)
    bo[...] = pall[0, 0, width : width + 8].astype(F32)
    stores[1].start()
    stores[3].start()
    gather(1)

    drain(tgot, nz - 1, t_sem.at[1])
    for k in range(slots):
        values = tgot[:, k].reshape(rows, EMB)
        tab_out[k] = (mm(hot[k], values) * scale).astype(BF16)
    stores[4].start()
    gathered(1)
    stores[2].start()

    drain(send, groups - 1, a_send.at[0])
    drain(rsend, groups - 1, r_sem.at[0])
    drain(xgot, nz - 1, x_sem.at[0])
    drain(bgot, nz - 1, b_sem.at[0])
    drain(s5, nz - 1, t_sem.at[0])
    for i in range(2):
        drain(pgot.at[i], groups - 1, p_sem.at[i, 0])
        drain(tally, (groups - 1) * piece, q_sem.at[i, 0])
        swap_copy(i).wait_send()
        late_copy(i).wait_send()
    for z in range(nz):
        sib_copy(z).wait_send()
    for step in range(half_ring):
        uv_copy(mp, 0, step).wait_send()
        rr_copy(mp, 0, step).wait_send()
        if step < half_ring - 1:
            uv_copy(mp, 1, step).wait_send()
            rr_copy(mp, 1, step).wait_send()
    for store in stores:
        store.wait()


def hand_over(wg, u, v, b, table, wg_out, u_out, v_out, b_out, table_out, sems):
    pairs = [(wg, wg_out), (u, u_out), (v, v_out), (table, table_out)]
    copies = [pltpu.make_async_copy(a, c, sems.at[i]) for i, (a, c) in enumerate(pairs)]
    for copy in copies:
        copy.start()
    b_out[...] = b[0:1, 0 : b_out.shape[1]]
    for copy in copies:
        copy.wait()


def on_device(
    cross_in,
    rank_act,
    tower_cot,
    tenant_ids,
    sparse_ids,
    table_slot,
    cross_u,
    cross_v,
    cross_bias,
    tower_w,
):
    nd, nt, nz = lax.axis_size("dp"), lax.axis_size("tenant"), lax.axis_size("mp")
    groups = nd * nt
    rows, width = cross_in.shape
    rank, hid = rank_act.shape[1], tower_cot.shape[1]
    tables = table_slot.shape[0]
    slots = (tables + nz - 1) // nz
    cap = (5 * rows + 4 * groups - 1) // (4 * groups)
    chunk = rows // nz
    half_ring = nz // 2
    scale = 1.0 / math.sqrt(rows * groups)

    anywhere = pl.BlockSpec(memory_space=pl.ANY)
    smem = pl.BlockSpec(memory_space=pltpu.SMEM)
    sem = pltpu.SemaphoreType.DMA

    def bf(*shape):
        return pltpu.VMEM(shape, BF16)

    def ff(*shape):
        return pltpu.VMEM(shape, F32)

    out = pl.pallas_call(
        functools.partial(fused, nd, nt, nz, cap, scale),
        out_shape=(
            jax.ShapeDtypeStruct((width, hid), BF16),
            jax.ShapeDtypeStruct((width, rank), F32),
            jax.ShapeDtypeStruct((width, rank), F32),
            jax.ShapeDtypeStruct((8, WIDE), F32),
            jax.ShapeDtypeStruct((slots, VOCAB, EMB), BF16),
        ),
        in_specs=[smem] + [anywhere] * 9,
        out_specs=(anywhere,) * 5,
        scratch_shapes=[
            pltpu.VMEM((1, rows), jnp.int32),
            bf(width, rows),
            bf(width, rank),
            bf(rows, rank),
            ff(1, width),
            bf(rows, hid),
            bf(width, rank),
            bf(width, hid),
            pltpu.VMEM((tables, rows), jnp.int32),
            bf(width, hid),
            bf(slots, VOCAB, EMB),
            pltpu.SMEM((nz * slots,), jnp.int32),
            sem((9,)),
            sem((5,)),
            ff(2, width, rank),
            ff(8, WIDE),
            bf(nz, 2, 2, WIDE, rank // 2),
            bf(2, WIDE, rank // 2),
            bf(2, WIDE, rank // 2),
            bf(WIDE, rows),
            bf(rows, WIDE),
            bf(rows, WIDE),
            bf(WIDE, hid),
            pltpu.VMEM((8, rows), jnp.int32),
            bf(rows, groups * cap),
            bf(groups, 2 * cap, hid // 2 + 128),
            bf(groups, 2 * cap, hid // 2 + 128),
            bf(groups * cap, hid),
            bf(groups * cap, WIDE),
            bf(groups, 2 * cap, 128),
            bf(groups, 2 * cap, 128),
            bf(groups * cap, WIDE),
            bf(rows, WIDE),
            bf(rows, WIDE),
            bf(nz, chunk, WIDE),
            bf(nz, chunk, WIDE),
            ff(nz, chunk, WIDE),
            bf(nz, chunk, rank),
            ff(nz, chunk, WIDE),
            bf(tables + 1, chunk, EMB),
            bf(nz, slots, chunk, EMB),
            bf(nz, slots, chunk, EMB),
            bf(slots, VOCAB, rows),
            ff(2, 2, WIDE, WIDE),
            ff(2, groups, 2 * WIDE // groups, WIDE),
            bf(2, 2 * WIDE // groups, WIDE),
            bf(2, 2, WIDE, WIDE),
            bf((groups - 1) * 2 * WIDE // groups, WIDE),
            sem((2,)),
            sem((nt // 2,)),
            sem((2,)),
            sem((2,)),
            sem((2,)),
            sem((2, 2, half_ring)),
            sem((2, nz)),
            sem((2, nz)),
            sem((2, nz)),
            sem((2,)),
            sem((2,)),
            sem((2,)),
            sem((2,)),
            sem((2, half_ring)),
            sem((nz,)),
            sem((2,)),
            sem((2, 2)),
            sem((2, 2)),
        ],
        compiler_params=pltpu.CompilerParams(
            collective_id=0, has_side_effects=True, vmem_limit_bytes=60 * 2**20
        ),
    )(
        table_slot,
        tenant_ids.T,
        cross_in.T,
        cross_u,
        rank_act,
        cross_bias[None, :],
        tower_cot,
        cross_v,
        tower_w[0],
        sparse_ids.T,
    )
    vmem = pl.BlockSpec(memory_space=pltpu.VMEM)
    wgrad, u_total, v_total, b_total, table = pl.pallas_call(
        hand_over,
        out_shape=tuple(
            jax.ShapeDtypeStruct((1, width) if i == 3 else x.shape, x.dtype)
            for i, x in enumerate(out)
        ),
        in_specs=[vmem] * 5,
        out_specs=(anywhere, anywhere, anywhere, vmem, anywhere),
        scratch_shapes=[sem((4,))],
    )(*out)
    return wgrad[None], u_total, v_total, b_total[0], table[None]


def solution(mesh):
    return jax.shard_map(
        on_device,
        mesh=mesh,
        in_specs=(
            P(("dp", "tenant"), "mp"),
            P(("dp", "tenant"), None),
            P(("dp", "tenant"), None),
            P(("dp", "tenant"), None),
            P(("dp", "tenant"), None),
            P(),
            P("mp", None),
            P("mp", None),
            P("mp"),
            P(("dp", "tenant"), "mp", None),
        ),
        out_specs=(
            P(("dp", "tenant"), "mp", None),
            P("mp", None),
            P("mp", None),
            P("mp"),
            P(("dp", "tenant"), "mp", None, None),
        ),
        check_vma=False,
    )
```

time: 214 us -> 177 us (0.83)
  Pallas kernels: 201 us -> 176 us
  local copies, waits for them, and re-layouts: 8.84 us -> 0 us
  other arithmetic: 2.84 us -> 0 us
    pallas_call x1, Pallas kernels: 201 us -> 173 us  [on_device(): pl.pallas_call(functools.partial(fused, nd, nt, nz, cap, scale), out_shap...]
    unnamed x10 -> x0, local copies, waits for them, and re-layouts: 8.84 us -> none
    pallas_call x0 -> x1, Pallas kernels: none -> 3.29 us  [on_device(): pl.pallas_call(hand_over, out_shape=tuple((jax.ShapeDtypeStruct((1, width...]
where the time goes in v2:
time: 177 us
  Pallas kernels  176 us (99%)
    pallas_call x1, Pallas kernels, on_device(): pl.pallas_call(functools.partial(fused, nd, nt, nz, cap, scale), out_shap...  173 us

profile of v2, /device:TPU:1, one launch (start us, length us, event | category | flops | bytes accessed | tf_op | source)
XLA Modules:
  0.0 176.8 jit_solution(2977634484425904668)
XLA Ops:
  0.6 172.9 %shard_map.137 = (bf16[216,1024]{1,0:T(8,128)(2,1)}, f32[216,512]{1,0:T(8,128)}, f32[216,512]{1,0:T(8,128)}, f32[8,256]{1,0:T(8,128)}, bf16[2,1024,128]{2,1,0:T(8,128)(2,1)}) custom-call(s32[26]{0:T(128)} %slot_ref.1, s32[1,1024]{1,0:T(1,128)} %bitcast.11, bf16[216,1024]{1,0:T(8,128)(2,1)} %bitcast.8, bf16[216,512]{1,0:T(8,128)(2,1)} %u_hbm.1, ...), custom_call_target="tpu_custom_call" | custom-call | tf_op jit(solution)/shard_map/pallas_call | solution.py:717
  173.5 3.3 %shard_map.138 = (bf16[216,1024]{1,0:T(8,128)(2,1)}, f32[216,512]{1,0:T(8,128)}, f32[216,512]{1,0:T(8,128)}, f32[1,216]{1,0:T(1,128)}, bf16[2,1024,128]{2,1,0:T(8,128)(2,1)}) custom-call(bf16[216,1024]{1,0:T(8,128)(2,1)} %get-tuple-element.15.wg, f32[216,512]{1,0:T(8,128)} %get-tuple-element.16.u, f32[216,512]{1,0:T(8,128)} %get-tuple-element.17.v, ...), custom_call_target="tpu_custom_call" | custom-call | tf_op jit(solution)/shard_map/pallas_call | solution.py:812

commit v3 on v2

--- a/solution.py
+++ b/solution.py
@@ -10,7 +10,7 @@
 
 EMB = 128
 VOCAB = 1024
-T_SENT = (2, 4, 6, 8, 12)
+T_SENT = (2, 4, 6, 8, 8)
 WIDE = 256
 MESH = pl.DeviceIdType.MESH
 F32 = jnp.float32
@@ -418,12 +418,12 @@
     def r_copy(peer):
         return remote(rsend.at[peer], rgot.at[me], r_sem.at[0], r_sem.at[1], plane(peer))
 
-    for step in range(4, half_ring + 1):
+    for step in range(4, half_ring - 1):
         uv_ring(step)
-    for i in range(2):
-        swap_copy(i).start()
-
-    each_z(lambda z: x_copy(z).start())
+        if step == half_ring - 3:
+            each_z(lambda z: x_copy(z).start())
+    if half_ring < 7:
+        each_z(lambda z: x_copy(z).start())
 
     def owner(k, carry):
         firsts = tenants_of(k, -1)
@@ -463,6 +463,8 @@
 
     lax.fori_loop(0, nx, owner, 0)
     rgot[me] = rsend[me]
+    if half_ring > 4:
+        uv_ring(half_ring - 1)
 
     wgrad = mm_tn(crr[...], cotr[...])
     wg_out[...] = (wgrad[0:width] * scale).astype(BF16)
@@ -532,6 +534,9 @@
     part[0, 0, width : width + 8] = mm(jnp.ones((8, rows), BF16), gate_h[...])
     scatter(0)
 
+    uv_ring(half_ring)
+    for i in range(2):
+        swap_copy(i).start()
     for z in range(nz):
         sib_copy(z).wait_recv()
 
@@ -565,31 +570,25 @@
     rr = jnp.concatenate([lo, up], axis=1).astype(BF16)
     rr_all[mp] = rr
 
-    def rr_copy(c, way, step):
-        return remote(
-            rr_all.at[c],
-            rr_all.at[c],
-            rr_send.at[way, step],
-            rr_recv.at[c],
-            column(right if way == 0 else left),
-        )
-
-    rr_copy(mp, 0, 0).start()
-    rr_copy(mp, 1, 0).start()
+    def rr_copy(c, way, step, i):
+        spot = rr_all.at[c, pl.ds(i * (chunk // 2), chunk // 2)]
+        to = column(right if way == 0 else left)
+        return remote(spot, spot, rr_send.at[i, way, step], rr_recv.at[i, c], to)
+
+    for i in range(2):
+        rr_copy(mp, 0, 0, i).start()
+        rr_copy(mp, 1, 0, i).start()
 
     def rr_ring(step):
         came = lax.rem(mp + nz - step, nz)
-        rr_copy(came, 0, step - 1).wait_recv()
-
-        @pl.when(step < half_ring)
-        def _():
-            rr_copy(came, 0, step).start()
-            other = lax.rem(mp + step, nz)
-            rr_copy(other, 1, step - 1).wait_recv()
-
-            @pl.when(step < half_ring - 1)
-            def _():
-                rr_copy(other, 1, step).start()
+        other = lax.rem(mp + step, nz)
+        for i in range(2):
+            rr_copy(came, 0, step - 1, i).wait_recv()
+            if step < half_ring:
+                rr_copy(came, 0, step, i).start()
+                rr_copy(other, 1, step - 1, i).wait_recv()
+            if step < half_ring - 1:
+                rr_copy(other, 1, step, i).start()
 
     def input_of(z, carry):
         igp[z] = bgot[z].astype(F32) * shift[z] + (
@@ -663,10 +662,12 @@
         sib_copy(z).wait_send()
     for step in range(half_ring):
         uv_copy(mp, 0, step).wait_send()
-        rr_copy(mp, 0, step).wait_send()
+        for i in range(2):
+            rr_copy(mp, 0, step, i).wait_send()
         if step < half_ring - 1:
             uv_copy(mp, 1, step).wait_send()
-            rr_copy(mp, 1, step).wait_send()
+            for i in range(2):
+                rr_copy(mp, 1, step, i).wait_send()
     for store in stores:
         store.wait()
 
@@ -787,8 +788,8 @@
             sem((2,)),
             sem((2,)),
             sem((2,)),
-            sem((2, half_ring)),
-            sem((nz,)),
+            sem((2, 2, half_ring)),
+            sem((2, nz)),
             sem((2,)),
             sem((2, 2)),
             sem((2, 2)),

time: 177 us -> 163 us (0.921)
  Pallas kernels: 176 us -> 161 us
    pallas_call x1, Pallas kernels: 173 us -> 158 us  [on_device(): pl.pallas_call(functools.partial(fused, nd, nt, nz, cap, scale), out_shap...]
where the time goes in v3:
time: 163 us; the launch traced here: 162 us
  Pallas kernels  161 us (99%)
    pallas_call x1, Pallas kernels, on_device(): pl.pallas_call(functools.partial(fused, nd, nt, nz, cap, scale), out_shap...  158 us
    pallas_call x1, Pallas kernels, on_device(): pl.pallas_call(hand_over, out_shape=tuple((jax.ShapeDtypeStruct((1, width...  3.29 us

profile of v3, /device:TPU:1, one launch (start us, length us, event | category | flops | bytes accessed | tf_op | source)
XLA Modules:
  0.0 161.6 jit_solution(6640552129420458237)
XLA Ops:
  0.6 157.7 %shard_map.137 = (bf16[216,1024]{1,0:T(8,128)(2,1)}, f32[216,512]{1,0:T(8,128)}, f32[216,512]{1,0:T(8,128)}, f32[8,256]{1,0:T(8,128)}, bf16[2,1024,128]{2,1,0:T(8,128)(2,1)}) custom-call(s32[26]{0:T(128)} %slot_ref.1, s32[1,1024]{1,0:T(1,128)} %bitcast.11, bf16[216,1024]{1,0:T(8,128)(2,1)} %bitcast.8, bf16[216,512]{1,0:T(8,128)(2,1)} %u_hbm.1, ...), custom_call_target="tpu_custom_call" | custom-call | tf_op jit(solution)/shard_map/pallas_call | solution.py:718
  158.3 3.3 %shard_map.138 = (bf16[216,1024]{1,0:T(8,128)(2,1)}, f32[216,512]{1,0:T(8,128)}, f32[216,512]{1,0:T(8,128)}, f32[1,216]{1,0:T(1,128)}, bf16[2,1024,128]{2,1,0:T(8,128)(2,1)}) custom-call(bf16[216,1024]{1,0:T(8,128)(2,1)} %get-tuple-element.15.wg, f32[216,512]{1,0:T(8,128)} %get-tuple-element.16.u, f32[216,512]{1,0:T(8,128)} %get-tuple-element.17.v, ...), custom_call_target="tpu_custom_call" | custom-call | tf_op jit(solution)/shard_map/pallas_call | solution.py:813

commit v4 on v3

--- a/solution.py
+++ b/solution.py
@@ -10,7 +10,7 @@
 
 EMB = 128
 VOCAB = 1024
-T_SENT = (2, 4, 6, 8, 8)
+T_SENT = (0, 2, 4, 4, 6)
 WIDE = 256
 MESH = pl.DeviceIdType.MESH
 F32 = jnp.float32

time: 163 us -> 162 us (level)
  no operation moved by 1% of the time
where the time goes in v4:
time: 162 us; the launch traced here: 161 us
  Pallas kernels  160 us (99%)
    pallas_call x1, Pallas kernels, on_device(): pl.pallas_call(functools.partial(fused, nd, nt, nz, cap, scale), out_shap...  157 us
    pallas_call x1, Pallas kernels, on_device(): pl.pallas_call(hand_over, out_shape=tuple((jax.ShapeDtypeStruct((1, width...  3.29 us

profile of v4, /device:TPU:1, one launch (start us, length us, event | category | flops | bytes accessed | tf_op | source)
XLA Modules:
  0.0 161.0 jit_solution(16142962345974020494)
XLA Ops:
  0.6 157.0 %shard_map.137 = (bf16[216,1024]{1,0:T(8,128)(2,1)}, f32[216,512]{1,0:T(8,128)}, f32[216,512]{1,0:T(8,128)}, f32[8,256]{1,0:T(8,128)}, bf16[2,1024,128]{2,1,0:T(8,128)(2,1)}) custom-call(s32[26]{0:T(128)} %slot_ref.1, s32[1,1024]{1,0:T(1,128)} %bitcast.11, bf16[216,1024]{1,0:T(8,128)(2,1)} %bitcast.8, bf16[216,512]{1,0:T(8,128)(2,1)} %u_hbm.1, ...), custom_call_target="tpu_custom_call" | custom-call | tf_op jit(solution)/shard_map/pallas_call | solution.py:718
  157.7 3.3 %shard_map.138 = (bf16[216,1024]{1,0:T(8,128)(2,1)}, f32[216,512]{1,0:T(8,128)}, f32[216,512]{1,0:T(8,128)}, f32[1,216]{1,0:T(1,128)}, bf16[2,1024,128]{2,1,0:T(8,128)(2,1)}) custom-call(bf16[216,1024]{1,0:T(8,128)(2,1)} %get-tuple-element.15.wg, f32[216,512]{1,0:T(8,128)} %get-tuple-element.16.u, f32[216,512]{1,0:T(8,128)} %get-tuple-element.17.v, ...), custom_call_target="tpu_custom_call" | custom-call | tf_op jit(solution)/shard_map/pallas_call | solution.py:813
